TPU v7x, 32 devices: a whole 2x2x4 slice. The times are simulated.
32 devices in a mesh: grp: 2 (over x), wide: 16 (over z, y, core).
Axes of the slice: x: 2, y: 2, z: 4, core: 2. Of those that a mesh axis runs over, the one named last changes fastest.
Arguments:
- homolog_stack_state: bfloat16 [256, 128, 256], P(('grp', 'wide')), parts along dimension 0, may hold values from -6 to 6
- present_flags: int32 [256, 128], P('grp'), parts along dimension 0, may hold values from 0 to 1, as said below
- chain_ordinal_labels: int32 [256], P('grp'), parts along dimension 0, may hold values from 0 to 383, as said below
- pairwise_repr: bfloat16 [256, 128, 128], P(('grp', 'wide')), parts along dimension 0, may hold values from -6 to 6
- heeding_normalizer_gains: float32 [256], replicated, may hold values from 0.1 to 1.9
- retrieval_weights_qkv: bfloat16 [256, 768], replicated, may hold values from -2.7308912 to 2.7308912
- logistic_weights: bfloat16 [256, 256], replicated, may hold values from -0.375 to 0.375
- logistic_intercept: float32 [256], replicated, may hold values from -4 to 4
- emitted_weights: bfloat16 [256, 256], replicated, may hold values from -0.375 to 0.375
- dyadic_normalizer_gains: float32 [256], replicated, may hold values from 0.1 to 1.9
- former_operand_weights: bfloat16 [256, 32], replicated, may hold values from -0.375 to 0.375
- latter_operand_weights: bfloat16 [256, 32], replicated, may hold values from -0.375 to 0.375
- flattened_outer_projection: bfloat16 [1024, 128], replicated, may hold values from -0.75 to 0.75
- clipped_separation_embedding: bfloat16 [65, 128], replicated, may hold values from -5 to 5
Outputs:
- homolog_changed: bfloat16 [256, 128, 256], P(('grp', 'wide')), parts along dimension 0
- couple_state_changed: bfloat16 [256, 128, 128], P(('grp', 'wide')), parts along dimension 0
There are 2 independent parts, one for each index of `grp`. A program takes and returns all parts, laid end to end along the dimension named above; an argument that names none is the same for every part. Nothing has to cross between parts.
Inputs may be any that keep to these rules, and one draw needn't show every extreme that they name: `present_flags`: every entry of the first sequence is 1. `chain_ordinal_labels`: rises from token to token by 1 to 3.
All inputs are finite; a program needn't handle non-finite values.
Results may differ from a plain program's by a relative error of at most 0.0094.
The roundings to bfloat16 on the way count: a program that leaves them out, or rounds other values in their place, can miss the bound.
Values may be sent and summed in bfloat16 or wider, within the bound.
A program may use at most 128 MiB of HBM per device.

v0:
```python
import math

import jax
import jax.numpy as jnp
from jax import lax
from jax.sharding import PartitionSpec as P

HEAD_TOTAL = 8
RELPOS_CLIP = 32
HEAD_SIZE = 32


epsilon = 1e-05


def standardize_features(values, gain_vector):
    mean = jnp.mean(values, axis=-1, keepdims=True)
    centered = values - mean
    variance = jnp.mean(centered * centered, axis=-1, keepdims=True)
    return centered * lax.rsqrt(variance + epsilon) * gain_vector


def downward_heeding_blend(
    homolog_stack_state,
    presence_tally,
    heeding_normalizer_gains,
    retrieval_weights_qkv,
    logistic_weights,
    logistic_intercept,
    emitted_weights,
):
    strand_lines, span_features, feature_count = homolog_stack_state.shape
    standardized_source = (
        standardize_features(homolog_stack_state.astype(jnp.float32), heeding_normalizer_gains)
        .astype(jnp.bfloat16)
        .reshape(strand_lines * span_features, feature_count)
    )
    packed = jnp.dot(
        standardized_source, retrieval_weights_qkv, preferred_element_type=jnp.float32
    ).astype(jnp.bfloat16)
    packed = packed.reshape(strand_lines, span_features, 3, HEAD_TOTAL, HEAD_SIZE)
    gate = jax.nn.sigmoid(
        jnp.dot(standardized_source, logistic_weights, preferred_element_type=jnp.float32)
        + logistic_intercept
    )
    gate = gate.reshape(strand_lines, span_features, feature_count)
    logits = jnp.einsum(
        "sthd,uthd->thsu", packed[:, :, 0], packed[:, :, 1], preferred_element_type=jnp.float32
    ) / math.sqrt(HEAD_SIZE)
    logits = logits + 1000000000.0 * (presence_tally.T[:, None, None, :] - 1.0)
    attn_weights = jax.nn.softmax(logits, axis=-1).astype(jnp.bfloat16)
    mixed = jnp.einsum(
        "thsu,uthd->sthd", attn_weights, packed[:, :, 2], preferred_element_type=jnp.float32
    ).reshape(strand_lines, span_features, feature_count)
    gated = (mixed * gate).astype(jnp.bfloat16).reshape(strand_lines * span_features, feature_count)
    increment_terms = jnp.dot(gated, emitted_weights, preferred_element_type=jnp.float32).reshape(
        strand_lines, span_features, feature_count
    )
    return (homolog_stack_state.astype(jnp.float32) + increment_terms).astype(jnp.bfloat16)


def map_operand_half(alignment_fresh, mask_portion, gain_vector, weight_matrix):
    strand_lines, span_features, feature_count = alignment_fresh.shape
    standardized_source = (
        standardize_features(alignment_fresh.astype(jnp.float32), gain_vector)
        .astype(jnp.bfloat16)
        .reshape(strand_lines * span_features, feature_count)
    )
    factor = jnp.dot(
        standardized_source, weight_matrix, preferred_element_type=jnp.float32
    ).reshape(strand_lines, span_features, weight_matrix.shape[1])
    return (factor * mask_portion[:, :, None]).astype(jnp.bfloat16)


def on_device(
    homolog_stack_state,
    present_flags,
    chain_ordinal_labels,
    pairwise_repr,
    heeding_normalizer_gains,
    retrieval_weights_qkv,
    logistic_weights,
    logistic_intercept,
    emitted_weights,
    dyadic_normalizer_gains,
    former_operand_weights,
    latter_operand_weights,
    flattened_outer_projection,
    clipped_separation_embedding,
):
    my_index = lax.axis_index("wide")
    whole_span_features = homolog_stack_state.shape[1]
    tok_local = pairwise_repr.shape[0]
    existence_overall = present_flags.astype(jnp.float32)
    presence_tally = lax.dynamic_slice_in_dim(existence_overall, my_index * tok_local, tok_local, 1)
    span_arrangement = lax.all_to_all(
        homolog_stack_state, "wide", split_axis=1, concat_axis=0, tiled=True
    )
    newest_symbol = downward_heeding_blend(
        span_arrangement,
        presence_tally,
        heeding_normalizer_gains,
        retrieval_weights_qkv,
        logistic_weights,
        logistic_intercept,
        emitted_weights,
    )
    homolog_changed = lax.all_to_all(newest_symbol, "wide", split_axis=0, concat_axis=1, tiled=True)
    left_tok = map_operand_half(
        newest_symbol, presence_tally, dyadic_normalizer_gains, former_operand_weights
    )
    pair_width = flattened_outer_projection.shape[1]
    right_tok = map_operand_half(
        newest_symbol, presence_tally, dyadic_normalizer_gains, latter_operand_weights
    )
    piece = lax.all_gather(right_tok, "wide", axis=1, tiled=True)
    width_j = piece.shape[1]
    outer = jnp.einsum("sic,sje->ijce", left_tok, piece, preferred_element_type=jnp.float32)
    outer = outer.astype(jnp.bfloat16).reshape(
        tok_local * width_j, flattened_outer_projection.shape[0]
    )
    projected = jnp.dot(
        outer, flattened_outer_projection, preferred_element_type=jnp.float32
    ).reshape(tok_local, width_j, pair_width)
    counts = jnp.dot(presence_tally.T, existence_overall, precision=lax.Precision.HIGHEST)
    increment_terms = projected / counts[:, :, None]
    span = 2 * RELPOS_CLIP + 1
    residue_mine = lax.dynamic_slice_in_dim(
        chain_ordinal_labels, my_index * tok_local, tok_local, 0
    )
    offsets = (
        jnp.clip(residue_mine[:, None] - chain_ordinal_labels[None, :], -RELPOS_CLIP, RELPOS_CLIP)
        + RELPOS_CLIP
    )
    one_hot = (offsets[:, :, None] == jnp.arange(span, dtype=jnp.int32)[None, None, :]).astype(
        jnp.bfloat16
    )
    relpos = jnp.dot(
        one_hot.reshape(tok_local * whole_span_features, span),
        clipped_separation_embedding,
        preferred_element_type=jnp.float32,
    )
    relpos = relpos.reshape(tok_local, whole_span_features, pair_width)
    couple_state_changed = (pairwise_repr.astype(jnp.float32) + relpos + increment_terms).astype(
        jnp.bfloat16
    )
    return (homolog_changed, couple_state_changed)


def solution(mesh):
    in_specs = (
        P(("grp", "wide"), None, None),
        P("grp", None),
        P("grp"),
        P(("grp", "wide"), None, None),
        P(),
        P(),
        P(),
        P(),
        P(),
        P(),
        P(),
        P(),
        P(),
        P(),
    )
    out_specs = (P(("grp", "wide"), None, None), P(("grp", "wide"), None, None))
    return jax.shard_map(
        on_device, mesh=mesh, in_specs=in_specs, out_specs=out_specs, check_vma=False
    )
```

profile of v0, /device:TPU:0, one launch (start us, length us, event | category | flops | bytes accessed | tf_op | source)
XLA Modules:
  0.0 122.4 jit_solution(15880398915262944570)
XLA Ops:
  7.2 2.2 %copy.73 = bf16[8,128,256]{2,0,1:T(8,128)(2,1)} copy(bf16[8,128,256]{2,1,0:T(8,128)(2,1)} %param.14) | data formatting | bytes 1048576 | tf_op args[0]
  9.4 7.4 %all-to-all-start = ((bf16[8,128,256]{2,0,1:T(8,128)(2,1)}), bf16[8,128,256]{2,0,1:T(8,128)(2,1)S(1)}, u32[]{:S(2)}, u32[]{:S(2)}) async-start(bf16[8,128,256]{2,0,1:T(8,128)(2,1)} %copy.73), calls=%async_computation | async-start | bytes 1048576 | tf_op jit(solution)/shard_map/all_to_all | solution.py:96
  16.8 0.0 all-gather.2.cloned.1.call-start
  16.8 0.8 convert_element_type.83
  17.7 0.1 multiply_bitcast_fusion
  17.8 0.1 copy.91
  17.9 13.3 %all-to-all-done = bf16[8,128,256]{2,0,1:T(8,128)(2,1)S(1)} async-done(((bf16[8,128,256]{2,0,1:T(8,128)(2,1)}), bf16[8,128,256]{2,0,1:T(8,128)(2,1)S(1)}, u32[]{:S(2)}, u32[]{:S(2)}) %all-to-all-start) | async-done | bytes 524320 | tf_op jit(solution)/shard_map/all_to_all | solution.py:96
  31.2 0.2 fusion.28
  31.4 0.1 copy.77
  31.5 0.1 copy.79
  31.6 0.1 copy.78
  31.7 0.4 multiply_reduce_fusion
  32.1 0.1 copy.80
  32.2 0.1 copy.81
  32.3 0.1 rsqrt.21
  32.4 0.1 convert_bitcast_fusion.1
  32.5 0.1 copy.76
  32.6 0.1 div.42
  32.8 0.3 fusion.27
  33.1 0.8 copy-done.1
  33.9 0.6 convolution_convert_fusion
  34.5 5.7 %reshape.136 = bf16[128,8,3,8,32]{4,3,2,1,0:T(8,128)(2,1)} reshape(bf16[1024,768]{1,0:T(8,128)(2,1)S(1)} %convolution_convert_fusion) | data formatting | bytes 3145728 | tf_op jit(solution)/shard_map/reshape | solution.py:41
  40.2 6.1 %fusion.48 = (bf16[128,8,1,8,32]{4,3,2,1,0:T(8,128)(2,1)}, bf16[128,8,1,8,32]{4,3,2,1,0:T(8,128)(2,1)}, bf16[128,8,1,8,32]{4,3,2,1,0:T(8,128)(2,1)}) fusion(bf16[128,8,3,8,32]{4,3,2,1,0:T(8,128)(2,1)} %reshape.136), kind=kLoop, calls=%fused_computation.69 | loop fusion | bytes 3145728 | tf_op jit(solution)/shard_map/slice | solution.py:53
  46.2 3.2 %copy.101 = bf16[128,8,1,8,32]{0,4,3,1,2:T(8,128)(2,1)S(1)} copy(bf16[128,8,1,8,32]{4,3,2,1,0:T(8,128)(2,1)} %get-tuple-element.5) | data formatting | bytes 1048576
  49.5 3.2 %copy.102 = bf16[128,8,1,8,32]{0,4,3,1,2:T(8,128)(2,1)S(1)} copy(bf16[128,8,1,8,32]{4,3,2,1,0:T(8,128)(2,1)} %get-tuple-element.6) | data formatting | bytes 1048576
  52.7 3.2 %copy.100 = bf16[128,8,1,8,32]{0,4,3,1,2:T(8,128)(2,1)S(1)} copy(bf16[128,8,1,8,32]{4,3,2,1,0:T(8,128)(2,1)} %get-tuple-element.4) | data formatting | bytes 1048576
  56.0 0.8 fusion.29
  56.7 2.0 %fusion.49 = (f32[8,8,128]{2,1,0:T(8,128)S(1)}, f32[8,8,128,128]{2,3,1,0:T(8,128)S(1)}) fusion(f32[8,8,128,128]{2,3,1,0:T(8,128)S(1)} %fusion.29, f32[8,128]{1,0:T(8,128)S(1)} %copy.85), kind=kOutput, calls=%fused_computation.70 | output fusion | flops 6291583 | bytes 8425472 | tf_op jit(solution)/shard_map/sub | solution.py:51
  58.7 0.7 fusion.5
  59.4 4.4 %copy.87 = f32[128,8,8,32]{3,2,1,0:T(8,128)} copy(f32[128,8,8,32]{0,3,2,1:T(8,128)S(1)} %fusion.5) | data formatting | bytes 2097152 | tf_op jit(solution)/shard_map/thsu,uthd->sthd/transpose | solution.py:52
  63.8 3.4 %reshape.137 = f32[1024,256]{1,0:T(8,128)S(1)} reshape(f32[128,8,8,32]{3,2,1,0:T(8,128)} %copy.87) | data formatting | bytes 2097152 | tf_op jit(solution)/shard_map/reshape | solution.py:54
  67.2 0.5 fusion.15
  67.8 0.8 convert_reduce_fusion
  68.6 0.4 fusion.21
  69.0 1.1 fusion.18
  70.1 0.0 all-gather.2.cloned.1.call-update
  70.2 1.1 copy.89
  71.2 4.1 %all-to-all-start.1 = ((bf16[128,8,256]{2,1,0:T(8,128)(2,1)}), bf16[128,8,256]{2,1,0:T(8,128)(2,1)S(1)}, u32[]{:S(2)}, u32[]{:S(2)}) async-start(bf16[128,8,256]{2,1,0:T(8,128)(2,1)} %copy.89), calls=%async_computation.1 | async-start | bytes 1048576 | tf_op jit(solution)/shard_map/all_to_all | solution.py:108
  75.4 0.1 dynamic_slice.7
  75.4 0.1 clamp_add_fusion
  75.5 0.2 fusion.45
  75.7 15.7 %all-to-all-done.1 = bf16[128,8,256]{2,1,0:T(8,128)(2,1)S(1)} async-done(((bf16[128,8,256]{2,1,0:T(8,128)(2,1)}), bf16[128,8,256]{2,1,0:T(8,128)(2,1)S(1)}, u32[]{:S(2)}, u32[]{:S(2)}) %all-to-all-start.1) | async-done | bytes 524320 | tf_op jit(solution)/shard_map/all_to_all | solution.py:108
  91.4 0.8 copy.114
  92.3 17.7 %all-gather.2.cloned.1.call-done = bf16[128,128,32]{0,2,1:T(8,128)(2,1)} async-done(((bf16[128,8,32]{0,2,1:T(8,128)(2,1)}), bf16[128,128,32]{0,2,1:T(8,128)(2,1)}) %all-gather.2.cloned.1.call-update) | async-done | bytes 1048592 | tf_op jit(solution)/shard_map/all_gather | solution.py:116
  110.0 2.3 %convert_bitcast_fusion = bf16[8,128,32,32]{1,2,0,3:T(8,128)(2,1)S(1)} fusion(bf16[128,128,32,1]{0,2,1,3:T(8,128)(2,1)} %bitcast.78, bf16[128,8,256]{2,0,1:T(8,128)(2,1)S(1)} %get-tuple-element.10, f32[256]{0:T(256)S(1)} %copy-done.10, f32[128,8]{0,1:T(8,128)S(1)} %add_rsqrt_fusion.1, f32[128,8]{0,1:T(8,128)S(1)} %broadcast_multiply_fusion.1, ...), kind=kOutput, calls=%fused_computation.5 | convolution fusion | flops 287637504 | bytes 3699712 | tf_op jit(solution)/shard_map/sic,sje->ijce/dot_general | solution.py:118
  112.3 1.4 %copy.93 = bf16[8,128,32,32]{1,3,2,0:T(8,128)(2,1)S(1)} copy(bf16[8,128,32,32]{1,2,0,3:T(8,128)(2,1)S(1)} %convert_bitcast_fusion) | data formatting | bytes 4194304 | tf_op jit(solution)/shard_map/convert_element_type | solution.py:119
  113.7 0.8 convolution_divide_fusion
  114.5 1.0 fusion.17
  (38 shorter events, 0.2 us)
Async XLA Ops:
  7.2 26.7 %copy-start = (bf16[256,768]{1,0:T(8,128)(2,1)S(1)}, bf16[256,768]{1,0:T(8,128)(2,1)}, u32[]{:S(2)}) copy-start(bf16[256,768]{1,0:T(8,128)(2,1)} %param.19) | copy-start | bytes 1179652
  7.2 25.6 %copy-start.11 = (f32[256]{0:T(256)S(1)}, f32[256]{0:T(256)}, u32[]{:S(2)}) copy-start(f32[256]{0:T(256)} %param.18) | copy-start | bytes 3076
  9.4 21.9 %all-to-all-start = ((bf16[8,128,256]{2,0,1:T(8,128)(2,1)}), bf16[8,128,256]{2,0,1:T(8,128)(2,1)S(1)}, u32[]{:S(2)}, u32[]{:S(2)}) async-start(bf16[8,128,256]{2,0,1:T(8,128)(2,1)} %copy.73), calls=%async_computation | async-start | bytes 1048576 | tf_op jit(solution)/shard_map/all_to_all | solution.py:96
  16.8 93.2 %all-gather.2.cloned.1.call-start = ((), (), s32[]{:S(2)}) async-start(), calls=%async_computation.2 | async-start | bytes 1114112 | tf_op jit(solution)/shard_map/all_gather | solution.py:116
  17.8 14.6 %copy-start.3 = (f32[128,8]{1,0:T(8,128)}, f32[128,8]{1,0:T(8,128)S(1)}, u32[]{:S(2)}) copy-start(f32[128,8]{1,0:T(8,128)S(1)} %get-tuple-element.3) | copy-start | bytes 12292
  33.1 0.8 copy-start.1
  59.4 7.8 %copy-start.2 = (bf16[1024,256]{1,0:T(8,128)(2,1)S(1)}, bf16[1024,256]{1,0:T(8,128)(2,1)}, u32[]{:S(2)}) copy-start(bf16[1024,256]{1,0:T(8,128)(2,1)} %copy-done.1) | copy-start | bytes 1572868
  59.4 7.8 %copy-start.14 = (bf16[256,256]{1,0:T(8,128)(2,1)S(1)}, bf16[256,256]{1,0:T(8,128)(2,1)}, u32[]{:S(2)}) copy-start(bf16[256,256]{1,0:T(8,128)(2,1)} %param.20) | copy-start | bytes 393220
  59.4 7.8 %copy-start.16 = (f32[256]{0:T(256)S(1)}, f32[256]{0:T(256)}, u32[]{:S(2)}) copy-start(f32[256]{0:T(256)} %param.21) | copy-start | bytes 3076
  63.8 3.9 %copy-start.7 = (bf16[256,256]{1,0:T(8,128)(2,1)S(1)}, bf16[256,256]{1,0:T(8,128)(2,1)}, u32[]{:S(2)}) copy-start(bf16[256,256]{1,0:T(8,128)(2,1)} %param.22) | copy-start | bytes 393220
  67.2 1.8 %copy-start.10 = (f32[256]{0:T(256)S(1)}, f32[256]{0:T(256)}, u32[]{:S(2)}) copy-start(f32[256]{0:T(256)} %param.23) | copy-start | bytes 3076
  67.2 1.8 %copy-start.15 = (bf16[256,32]{0,1:T(8,128)(2,1)S(1)}, bf16[256,32]{0,1:T(8,128)(2,1)}, u32[]{:S(2)}) copy-start(bf16[256,32]{0,1:T(8,128)(2,1)} %param.25) | copy-start | bytes 49156
  67.7 7.6 %copy-start.12 = (s32[128]{0:T(128)S(1)}, s32[128]{0:T(128)}, u32[]{:S(2)}) copy-start(s32[128]{0:T(128)} %param.16) | copy-start | bytes 1540
  67.7 7.8 %copy-start.4 = (f32[128,8]{1,0:T(8,128)S(1)}, f32[128,8]{1,0:T(8,128)}, u32[]{:S(2)}) copy-start(f32[128,8]{1,0:T(8,128)} %copy-done.3) | copy-start | bytes 12292
  67.7 7.8 %copy-start.5 = (s32[128,128]{1,0:T(8,128)S(1)}, s32[128,128]{1,0:T(8,128)}, u32[]{:S(2)}) copy-start(s32[128,128]{1,0:T(8,128)} %param.15) | copy-start | bytes 196612
  67.8 42.2 %copy-start.9 = (bf16[256,32]{0,1:T(8,128)(2,1)S(1)}, bf16[256,32]{0,1:T(8,128)(2,1)}, u32[]{:S(2)}) copy-start(bf16[256,32]{0,1:T(8,128)(2,1)} %param.24) | copy-start | bytes 49156
  71.2 20.2 %all-to-all-start.1 = ((bf16[128,8,256]{2,1,0:T(8,128)(2,1)}), bf16[128,8,256]{2,1,0:T(8,128)(2,1)S(1)}, u32[]{:S(2)}, u32[]{:S(2)}) async-start(bf16[128,8,256]{2,1,0:T(8,128)(2,1)} %copy.89), calls=%async_computation.1 | async-start | bytes 1048576 | tf_op jit(solution)/shard_map/all_to_all | solution.py:108
  92.3 21.4 %copy-start.13 = (bf16[1024,128]{1,0:T(8,128)(2,1)S(1)}, bf16[1024,128]{1,0:T(8,128)(2,1)}, u32[]{:S(2)}) copy-start(bf16[1024,128]{1,0:T(8,128)(2,1)} %param.26) | copy-start | bytes 786436
  112.3 2.2 %copy-start.6 = (bf16[8,128,128]{2,1,0:T(8,128)(2,1)S(1)}, bf16[8,128,128]{2,1,0:T(8,128)(2,1)}, u32[]{:S(2)}) copy-start(bf16[8,128,128]{2,1,0:T(8,128)(2,1)} %param.17) | copy-start | bytes 786436
  112.3 2.2 %copy-start.8 = (bf16[65,128]{1,0:T(8,128)(2,1)S(1)}, bf16[65,128]{1,0:T(8,128)(2,1)}, u32[]{:S(2)}) copy-start(bf16[65,128]{1,0:T(8,128)(2,1)} %param.27) | copy-start | bytes 49924
Sparse Core Ops, SparseCore 0:
  70.3 39.6 all-gather.1
where the time goes:
time: 123 us; the launch traced here: 122 us
  waiting for transfers between devices  46.8 us (38%)
  local copies, waits for them, and re-layouts  36.5 us (30%)
  between operations  14.4 us (12%)
  starting transfers between devices  11.5 us (9%)
  matrix products  8.73 us (7%)
  other arithmetic  4.44 us (4%)
    all_gather x1, waiting for transfers between devices, on_device(): piece = lax.all_gather(right_tok, 'wide', axis=1, tiled=True)  17.7 us
    all_to_all x1, waiting for transfers between devices, on_device(): lax.all_to_all(newest_symbol, 'wide', split_axis=0, concat_axis=1, tiled=...  15.7 us
    all_to_all x1, waiting for transfers between devices, on_device(): lax.all_to_all(homolog_stack_state, 'wide', split_axis=1, concat_axis=0,...  13.3 us
    unnamed x38, local copies, waits for them, and re-layouts  12.8 us
    all_to_all x1, starting transfers between devices, on_device(): lax.all_to_all(homolog_stack_state, 'wide', split_axis=1, concat_axis=0,...  7.39 us
    slice x1, local copies, waits for them, and re-layouts, downward_heeding_blend(): packed[:, :, 2]  6.06 us
    reshape x1, local copies, waits for them, and re-layouts, downward_heeding_blend(): packed.reshape(strand_lines, span_features, 3, HEAD_TOTAL, HEAD_SIZE)  5.69 us
    transpose x1, local copies, waits for them, and re-layouts, downward_heeding_blend(): jnp.einsum('thsu,uthd->sthd', attn_weights, packed[:, :, 2], preferred_el...  4.42 us
  transfers between devices with their start and end apart: 3, of which 3 were waited for; matrix products, arithmetic and copies ran while one was open for 3% of the time, Pallas kernels for 0%

commit v1 on v0

v1 whole, which is shorter than its diff:
```python
import functools
import math

import jax
import jax.numpy as jnp
from jax import lax
from jax.experimental import pallas as pl
from jax.experimental.pallas import tpu as pltpu
from jax.sharding import PartitionSpec as P

HEADS = 8
CLIP = 32
HEAD_SIZE = 32
CHUNK = 2
EPS = 1e-05
MESH = pl.DeviceIdType.MESH
F32 = jnp.float32
BF16 = jnp.bfloat16


def mm(a, b):
    return jnp.dot(a, b, preferred_element_type=F32)


def mm_nt(a, b):
    return lax.dot_general(a, b, (((1,), (1,)), ((), ())), preferred_element_type=F32)


def normalise(v, gain):
    mean = jnp.mean(v, axis=-1, keepdims=True)
    centred = v - mean
    var = jnp.mean(centred * centred, axis=-1, keepdims=True)
    return (centred * lax.rsqrt(var + EPS) * gain).astype(BF16)


def kernel(
    n, xs, flags, res_s, res_row, pair, g1, wqkv, wgate, bgate, wout, g2, wl, wr, wp, emb,
    ret, out,
    recv, ybuf, wt, wgb, wk_s, wl4, wrt, mcol, mrow, base, rcount, embp, pmat, rt, rb, obuf,
    a_send, a_recv, r_send, r_recv, g_send, gz, gy, gc,
):
    grp = lax.axis_index("grp")
    me = lax.axis_index("wide")
    tl, _, sl, ch = recv.shape
    tokens = flags.shape[1]
    seqs = flags.shape[0]
    nchunk = tl // CHUNK
    lanes = 128
    width = wl.shape[1]
    per = lanes // width

    barrier = pltpu.get_barrier_semaphore()

    def greet(d, carry):
        p = lax.rem(me + d, n)
        pl.semaphore_signal(barrier, inc=1, device_id=(grp, p), device_id_type=MESH)
        return carry

    lax.fori_loop(1, n, greet, 0)
    pl.semaphore_wait(barrier, n - 1)

    def send_chunk(k):
        part = pl.ds(k * CHUNK, CHUNK)
        pltpu.make_async_copy(xs.at[me, part], recv.at[part, me], a_recv.at[k]).start()

        def one(d, carry):
            p = lax.rem(me + d, n)
            pltpu.make_async_remote_copy(
                src_ref=xs.at[p, part], dst_ref=recv.at[part, me],
                send_sem=a_send, recv_sem=a_recv.at[k],
                device_id=(grp, p), device_id_type=MESH,
            ).start()
            return carry

        lax.fori_loop(1, n, one, 0)

    for k in range(nchunk):
        send_chunk(k)

    for a, src in ((0, wqkv[:, 0:ch]), (1, wqkv[:, 2 * ch : 3 * ch]), (2, wgate[...])):
        wt[a * ch : (a + 1) * ch, :] = src.astype(F32).T.astype(BF16)
    wgb[...] = jnp.broadcast_to(bgate[...], (lanes, ch)).T
    spread = (
        lax.broadcasted_iota(jnp.int32, (width, lanes), 1) % width
        == lax.broadcasted_iota(jnp.int32, (width, lanes), 0)
    ).astype(BF16)
    first = (
        lax.broadcasted_iota(jnp.int32, (width, lanes), 1)
        == lax.broadcasted_iota(jnp.int32, (width, lanes), 0)
    ).astype(BF16)
    wl4[...] = mm(wl[...], spread).astype(BF16)
    wrt[...] = mm(wr[...], first).T[0:width].astype(BF16)
    m_all = flags[...].astype(F32).astype(BF16)
    pick = (
        lax.broadcasted_iota(jnp.int32, (tokens, tl * lanes), 0)
        == me * tl + lax.broadcasted_iota(jnp.int32, (tokens, tl * lanes), 1) // lanes
    ).astype(F32).astype(BF16)
    mine = mm(m_all, pick)
    mcol[...] = mine
    pick8 = (
        lax.broadcasted_iota(jnp.int32, (tl, tokens), 1)
        == me * tl + lax.broadcasted_iota(jnp.int32, (tl, tokens), 0)
    ).astype(F32).astype(BF16)
    mrow[...] = mm_nt(pick8, m_all)
    embp[...] = jnp.zeros_like(embp)
    embp[0 : emb.shape[0], :] = emb[...].astype(F32)
    table = embp[...].astype(BF16)
    mine_b = mine.astype(BF16)
    for jb in range(tokens // lanes):
        js = slice(jb * lanes, (jb + 1) * lanes)
        mt = flags[:, js].astype(F32).T.astype(BF16)
        rcount[js, :] = 1.0 / mm(mt, mine_b)
        res_j = jnp.broadcast_to(res_row[0:1, js], (lanes, lanes)).T
        for i in range(tl):
            off = jnp.clip(res_s[me * tl + i] - res_j, -CLIP, CLIP) + CLIP
            hot = (off == lax.broadcasted_iota(jnp.int32, (lanes, lanes), 1)).astype(F32)
            base[i, js, :] = pair[i, js, :].astype(F32) + mm(hot.astype(BF16), table)

    gain1, gain2 = g1[...], g2[...]
    scale = math.log2(math.e) / math.sqrt(HEAD_SIZE)
    group = lanes // HEAD_SIZE
    lane_block = lax.broadcasted_iota(jnp.int32, (seqs, lanes), 1) // width

    def attend(k, carry):
        part = pl.ds(k * CHUNK, CHUNK)
        pltpu.make_async_copy(recv.at[part], recv.at[part], a_recv.at[k]).wait()
        x = recv[part].astype(F32).reshape(CHUNK * seqs, ch)
        nb = normalise(x, gain1)
        pt = mm_nt(wt[...], nb)
        keys = mm(nb, wqkv[:, ch : 2 * ch]).astype(BF16)
        qt = pt[0:ch].astype(BF16)
        vt = pt[ch : 2 * ch].astype(BF16)
        mixed_parts = []
        for t in range(CHUNK):
            ts = slice(t * seqs, (t + 1) * seqs)
            at = pl.ds(pl.multiple_of((k * CHUNK + t) * lanes, lanes), lanes)
            bias = (mcol[:, at] - 1.0) * 1e9
            gate = jax.nn.sigmoid(pt[2 * ch : 3 * ch, ts] + wgb[...])
            heads = []
            for g in range(HEADS // group):
                kg = keys[ts, g * lanes : (g + 1) * lanes]
                for h in range(group):
                    r = (g * group + h) * HEAD_SIZE
                    pieces = []
                    if h > 0:
                        pieces.append(jnp.zeros((h * HEAD_SIZE, seqs), BF16))
                    pieces.append(qt[r : r + HEAD_SIZE, ts])
                    if h < group - 1:
                        pieces.append(jnp.zeros(((group - 1 - h) * HEAD_SIZE, seqs), BF16))
                    logits = mm(kg, jnp.concatenate(pieces, axis=0)) * scale + bias
                    top = jnp.max(logits, axis=0, keepdims=True)
                    e = jnp.exp2(logits - top)
                    w = (e * (1.0 / jnp.sum(e, axis=0, keepdims=True))).astype(BF16)
                    heads.append(mm(vt[r : r + HEAD_SIZE, ts], w))
            mixed = jnp.concatenate(heads, axis=0)
            mixed_parts.append((mixed * gate).T.astype(BF16))
        gated = jnp.concatenate(mixed_parts, axis=0)
        y = (x + mm(gated, wout[...])).astype(BF16)
        yf = y.astype(F32)
        ybuf[part] = yf.reshape(CHUNK, n, sl, ch).astype(BF16)
        n2 = normalise(yf, gain2)
        left = mm(n2, wl4[...])
        right = mm_nt(wrt[...], n2)
        for t in range(CHUNK):
            ts = slice(t * seqs, (t + 1) * seqs)
            i = k * CHUNK + t
            at = pl.ds(pl.multiple_of(i * lanes, lanes), lanes)
            lt = left[ts] * mcol[:, at]
            for b in range(per):
                pmat[k, b * seqs : (b + 1) * seqs, t * lanes : (t + 1) * lanes] = jnp.where(
                    lane_block == b, lt, 0.0
                ).astype(BF16)
            rt[i] = right[:, ts] * mrow[pl.ds(i, 1), :]
        return carry

    def give_back(k):
        part = pl.ds(k * CHUNK, CHUNK)
        pltpu.make_async_copy(ybuf.at[part, me], ret.at[me, part], r_recv).start()

        def one(d, carry):
            p = lax.rem(me + d, n)
            pltpu.make_async_remote_copy(
                src_ref=ybuf.at[part, p], dst_ref=ret.at[me, part],
                send_sem=r_send, recv_sem=r_recv,
                device_id=(grp, p), device_id_type=MESH,
            ).start()
            return carry

        lax.fori_loop(1, n, one, 0)

    def attend_and_send(k, carry):
        attend(k, 0)
        give_back(k)
        return carry

    lax.fori_loop(0, nchunk - 1, attend_and_send, 0)
    attend(nchunk - 1, 0)

    lines = n // 4
    line, side, core = me // 4, lax.rem(me // 2, 2), lax.rem(me, 2)
    beside = line * 4 + (1 - side) * 2 + core
    twin = line * 4 + side * 2 + (1 - core)
    rb[me] = jnp.swapaxes(rt[...], 0, 1).astype(BF16)

    def push(block, to, sem):
        pltpu.make_async_remote_copy(
            src_ref=rb.at[block], dst_ref=rb.at[block], send_sem=g_send, recv_sem=sem,
            device_id=(grp, to), device_id_type=MESH,
        ).start()

    def along(d, carry):
        to = lax.rem(line + d, lines)
        push(me, to * 4 + side * 2 + core, gz.at[line])
        return carry

    push(me, beside, gy.at[line])
    lax.fori_loop(1, lines, along, 0)
    push(me, twin, gc)
    give_back(nchunk - 1)

    def pass_on(d, carry):
        at = lax.rem(line + d, lines)
        block = at * 4 + side * 2 + core
        pltpu.make_async_copy(rb.at[block], rb.at[block], gz.at[at]).wait()
        push(block, beside, gy.at[at])
        push(block, twin, gc)
        return carry

    lax.fori_loop(1, lines, pass_on, 0)

    def pass_side(d, carry):
        at = lax.rem(line + d, lines)
        block = at * 4 + (1 - side) * 2 + core
        pltpu.make_async_copy(rb.at[block], rb.at[block], gy.at[at]).wait()
        push(block, twin, gc)
        return carry

    lax.fori_loop(0, lines, pass_side, 0)
    half = rb.at[pl.ds(0, n // 2)]
    pltpu.make_async_copy(half, half, gc).wait()

    blocks = lanes // tl

    def pair_block(jb, carry):
        rows = pl.ds(pl.multiple_of(jb * lanes, lanes), lanes)
        for g in range(width // per):
            lhs = jnp.concatenate(
                [
                    rb[pl.ds(jb * blocks, blocks), g * per + b].astype(F32).reshape(lanes, seqs)
                    for b in range(per)
                ],
                axis=1,
            ).astype(BF16)
            for k in range(nchunk):
                o = mm(lhs, pmat[k]).astype(BF16)
                for t in range(CHUNK):
                    obuf[k * CHUNK + t, :, g * lanes : (g + 1) * lanes] = o[
                        :, t * lanes : (t + 1) * lanes
                    ]
        for i in range(tl):
            proj = mm(obuf[i], wp[...])
            out[i, rows, :] = (
                base[i, rows, :] + proj * rcount[rows, i * lanes : (i + 1) * lanes]
            ).astype(BF16)
        return carry

    lax.fori_loop(0, tokens // lanes, pair_block, 0)

    others = xs.at[pl.ds(0, n - 1)]
    pltpu.make_async_copy(others, others, a_send).wait()
    sent = rb.at[pl.ds(0, n - 1)]
    pltpu.make_async_copy(sent, sent, g_send).wait()
    pltpu.make_async_copy(others, others, r_send).wait()
    pltpu.make_async_copy(ret, ret, r_recv).wait()


def on_device(n, x, flags, res, pair, g1, wqkv, wgate, bgate, wout, g2, wl, wr, wp, emb):
    sl, tokens, ch = x.shape
    tl = pair.shape[0]
    seqs = flags.shape[0]
    width = wl.shape[1]
    lanes = 128
    pw = wp.shape[1]
    xs = x.reshape(sl, n, tl, ch).transpose(1, 2, 0, 3)
    wp2 = wp.reshape(width, width, pw).transpose(1, 0, 2).reshape(width * width, pw)
    vmem = pl.BlockSpec(memory_space=pltpu.VMEM)
    anyspace = pl.BlockSpec(memory_space=pl.ANY)
    smem = pl.BlockSpec(memory_space=pltpu.SMEM)
    nchunk = tl // CHUNK
    per = lanes // width
    dma = pltpu.SemaphoreType.DMA
    ret, out = pl.pallas_call(
        functools.partial(kernel, n),
        out_shape=(
            jax.ShapeDtypeStruct((n, tl, sl, ch), BF16),
            jax.ShapeDtypeStruct((tl, tokens, pw), BF16),
        ),
        in_specs=[anyspace, vmem, smem] + [vmem] * 12,
        out_specs=(anyspace, vmem),
        scratch_shapes=[
            pltpu.VMEM((tl, n, sl, ch), BF16),
            pltpu.VMEM((tl, n, sl, ch), BF16),
            pltpu.VMEM((3 * ch, ch), BF16),
            pltpu.VMEM((ch, lanes), F32),
            pltpu.VMEM((8, lanes), F32),
            pltpu.VMEM((ch, lanes), BF16),
            pltpu.VMEM((width, ch), BF16),
            pltpu.VMEM((seqs, tl * lanes), F32),
            pltpu.VMEM((tl, seqs), F32),
            pltpu.VMEM((tl, tokens, pw), F32),
            pltpu.VMEM((tokens, tl * lanes), F32),
            pltpu.VMEM((lanes, pw), F32),
            pltpu.VMEM((nchunk, per * seqs, CHUNK * lanes), BF16),
            pltpu.VMEM((tl, width, seqs), F32),
            pltpu.VMEM((n, width, tl, seqs), BF16),
            pltpu.VMEM((tl, lanes, width * width), BF16),
            dma, dma((nchunk,)), dma, dma, dma, dma((n // 4,)), dma((n // 4,)), dma,
        ],
        compiler_params=pltpu.CompilerParams(
            collective_id=0, has_side_effects=True, vmem_limit_bytes=56 * 1024 * 1024
        ),
        cost_estimate=pl.CostEstimate(
            flops=4 * 10**9, bytes_accessed=4 * 10**6, transcendentals=2 * 10**6
        ),
    )(
        xs, flags, res, res.reshape(1, tokens), pair, g1.reshape(1, ch), wqkv, wgate,
        bgate.reshape(1, ch), wout, g2.reshape(1, ch), wl, wr, wp2, emb,
    )
    changed = ret.transpose(2, 0, 1, 3).reshape(sl, tokens, ch)
    return changed, out


def solution(mesh):
    rows = P(("grp", "wide"), None, None)
    in_specs = (rows, P("grp", None), P("grp"), rows) + (P(),) * 10
    return jax.shard_map(
        functools.partial(on_device, mesh.shape["wide"]), mesh=mesh,
        in_specs=in_specs, out_specs=(rows, rows), check_vma=False,
    )
```

time: 123 us -> 53.2 us (0.43)
  waiting for transfers between devices: 46.8 us -> 0 us
  Pallas kernels: 0 us -> 43.6 us
  local copies, waits for them, and re-layouts: 36.5 us -> 8.48 us
  between operations: 14.4 us -> 0.66 us
  starting transfers between devices: 11.5 us -> 0 us
  matrix products: 8.73 us -> 0 us
  other arithmetic: 4.44 us -> 0 us
    pallas_call x0 -> x1, Pallas kernels: none -> 43.6 us  [on_device(): pl.pallas_call(functools.partial(kernel, n), out_shape=(jax.ShapeDtypeStr...]
    all_to_all x2 -> x0, waiting for transfers between devices: 29 us -> none  [the longest x1 15.7 us: on_device(): lax.all_to_all(newest_symbol, 'wide', split_axis=0, concat_axis=1, tiled=...]
    all_gather x1 -> x0, waiting for transfers between devices: 17.7 us -> none  [on_device(): piece = lax.all_gather(right_tok, 'wide', axis=1, tiled=True)]
    all_to_all x2 -> x0, starting transfers between devices: 11.5 us -> none  [the longest x1 7.39 us: on_device(): lax.all_to_all(homolog_stack_state, 'wide', split_axis=1, concat_axis=0,...]
    dot_general x10 -> x0, matrix products: 8.73 us -> none  [the longest x1 2.33 us: on_device(): jnp.einsum('sic,sje->ijce', left_tok, piece, preferred_element_type=jnp.f...]
    reshape x2 -> x1, local copies, waits for them, and re-layouts: 9.07 us -> 1.76 us  [on_device(): wp.reshape(width, width, pw).transpose(1, 0, 2).reshape(width * width, pw)]
    unnamed x38 -> x9, local copies, waits for them, and re-layouts: 12.8 us -> 6.73 us
    slice x1 -> x0, local copies, waits for them, and re-layouts: 6.06 us -> none  [downward_heeding_blend(): packed[:, :, 2]]
  transfers between devices with their start and end apart: 3 -> 0, of which waited for: 3 -> 0; matrix products, arithmetic and copies ran while one was open for 3% -> 0% of each run, Pallas kernels for 0% -> 0%
where the time goes in v1:
time: 53.2 us; the launch traced here: 52.7 us
  Pallas kernels  43.6 us (82%)
  local copies, waits for them, and re-layouts  8.48 us (16%)
  between operations  0.66 us (1%)
    pallas_call x1, Pallas kernels, on_device(): pl.pallas_call(functools.partial(kernel, n), out_shape=(jax.ShapeDtypeStr...  43.6 us
    unnamed x9, local copies, waits for them, and re-layouts  6.73 us
    reshape x1, local copies, waits for them, and re-layouts, on_device(): wp.reshape(width, width, pw).transpose(1, 0, 2).reshape(width * width, pw)  1.76 us

profile of v1, /device:TPU:0, one launch (start us, length us, event | category | flops | bytes accessed | tf_op | source)
XLA Modules:
  0.0 52.7 jit_solution(3530190004768869387)
XLA Ops:
  0.6 0.0 copy-start
  0.6 1.5 %copy.18.wl = bf16[256,32]{1,0:T(8,128)(2,1)} copy(bf16[256,32]{0,1:T(8,128)(2,1)} %param.24) | data formatting | bytes 32768 | tf_op args[10]
  2.2 1.4 %copy.19.wr = bf16[256,32]{1,0:T(8,128)(2,1)} copy(bf16[256,32]{0,1:T(8,128)(2,1)} %param.25) | data formatting | bytes 32768 | tf_op args[11]
  3.6 1.8 %copy.17 = bf16[32,32,128]{2,0,1:T(8,128)(2,1)} copy(bf16[32,32,128]{2,1,0:T(8,128)(2,1)} %bitcast.16) | data formatting | bytes 524288 | tf_op jit(solution)/shard_map/reshape | solution.py:285
  5.3 0.0 copy-done
  5.4 1.1 %copy.16 = bf16[8,128,256]{2,0,1:T(8,128)(2,1)} copy(bf16[8,128,256]{2,1,0:T(8,128)(2,1)S(1)} %copy-done) | data formatting | bytes 1048576 | tf_op args[0]
  6.4 43.6 %shard_map.149 = (bf16[16,8,8,256]{3,2,1,0:T(8,128)(2,1)}, bf16[8,128,128]{2,1,0:T(8,128)(2,1)}) custom-call(bf16[16,8,8,256]{3,2,1,0:T(8,128)(2,1)} %bitcast.15, s32[128,128]{1,0:T(8,128)} %flags.1, s32[128]{0:T(128)} %res_s.1, s32[1,128]{1,0:T(1,128)} %bitcast.21, bf16[8,128,128]{2,1,0:T(8,128)(2,1)} %pair.1, f32[1,256]{1,0:T(1,128)} %bitcast.18, ...), custom_call_target="tpu_custom_call" | custom-call | flops 4000000000 | bytes 4000000 | tf_op jit(solution)/shard_map/pallas_call | solution.py:292
  50.0 0.0 copy-start.1
  50.0 2.0 %copy.20 = bf16[8,128,256]{2,1,0:T(8,128)(2,1)} copy(bf16[8,128,256]{2,0,1:T(8,128)(2,1)} %bitcast.14) | data formatting | bytes 1048576
  52.0 0.0 copy-done.1
  52.0 0.7 %copy.22 = bf16[8,128,128]{2,1,0:T(8,128)(2,1)} copy(bf16[8,128,128]{2,1,0:T(8,128)(2,1)S(1)} %copy-done.1) | data formatting | bytes 524288
Async XLA Ops:
  0.6 4.7 %copy-start = (bf16[8,128,256]{2,1,0:T(8,128)(2,1)S(1)}, bf16[8,128,256]{2,1,0:T(8,128)(2,1)}, u32[]{:S(2)}) copy-start(bf16[8,128,256]{2,1,0:T(8,128)(2,1)} %param.14) | copy-start | bytes 1572868
  50.0 2.0 %copy-start.1 = (bf16[8,128,128]{2,1,0:T(8,128)(2,1)S(1)}, bf16[8,128,128]{2,1,0:T(8,128)(2,1)}, u32[]{:S(2)}) copy-start(bf16[8,128,128]{2,1,0:T(8,128)(2,1)} %get-tuple-element.11) | copy-start | bytes 786436
